TPU v7x, 512 devices: a whole 4x8x8 slice. The times are simulated.
512 devices in a mesh: tm: 16 (over y, core), nin: 8 (over z), nout: 4 (over x).
Axes of the slice: x: 4, y: 8, z: 8, core: 2. Of those that a mesh axis runs over, the one named last changes fastest.
Arguments:
- spikes: int32 [4096, 2048], P('tm', 'nin'), may hold values 0 or 1
- exposure: int32 [4096], P('tm'), may hold values from 1 to 8
- weights: bfloat16 [16384, 2048], P('nin', 'nout'), may hold values from -0.375 to 0.375
- direction: float32 [16384, 2048], P(('nin', 'tm'), 'nout'), may hold values from -6 to 6
- residual: float32 [16384, 2048], P(('nin', 'tm'), 'nout'), may hold values from -0.75 to 0.75
- iterate: float32 [16384, 2048], P(('nin', 'tm'), 'nout'), may hold values from -1.8 to 1.8
Outputs:
- new_iterate: float32 [16384, 2048], P(('nin', 'tm'), 'nout')
- new_residual: float32 [16384, 2048], P(('nin', 'tm'), 'nout')
- new_direction: float32 [16384, 2048], P(('nin', 'tm'), 'nout')
All inputs are finite; a program needn't handle non-finite values. No bound on the sum of `spikes` on one device may be relied on, other than what follows from the above.
Results may differ from a plain program's by a relative error of at most 0.015.
Values may be sent and summed in bfloat16 or wider, within the bound.
A program may use at most 64 MiB of HBM per device.

v0:
```python
import math
import jax
import jax.numpy as jnp
from jax import lax
from jax.sharding import PartitionSpec as P

BASES = 8
HISTORY = 128
RIDGE_WEIGHT = 0.05
NORM_EPS = 1e-06


def shifted(value, axis, steps):
    count = lax.axis_size(axis)
    initial, last = (max(0, -steps), min(count, count - steps))
    return lax.ppermute(value, axis, [(source, source + steps) for source in range(initial, last)])


def basis_table(history, bases_count):
    lag_values = jnp.arange(1, history + 1, dtype=jnp.float32)
    warped = jnp.log(lag_values + 1.0)
    log_low = math.log(2.0)
    log_high = math.log(history + 1.0)
    spacing = (log_high - log_low) / (bases_count - 1)
    centers = log_low + spacing * jnp.arange(bases_count, dtype=jnp.float32)
    phases = (warped[:, None] - centers[None, :]) * (math.pi / (2.0 * spacing))
    phases = jnp.clip(phases, -math.pi, math.pi)
    bump_values = 0.5 * (1.0 + jnp.cos(phases))
    bump_values = bump_values / jnp.sum(bump_values, axis=0, keepdims=True)
    return bump_values.astype(jnp.bfloat16)


def lag_kernel(basis_rows, span, offset):
    out_index = jnp.arange(span, dtype=jnp.int32)[:, None]
    in_index = jnp.arange(span, dtype=jnp.int32)[None, :]
    lag_index = out_index + offset - in_index
    is_valid = (lag_index >= 1) & (lag_index <= HISTORY)
    take_index = jnp.clip(lag_index - 1, 0, HISTORY - 1)
    return jnp.where(
        is_valid[None], jnp.take(basis_rows.T, take_index, axis=1), jnp.zeros((), jnp.bfloat16)
    )


def per_device(spikes, exposure, weights, direction, residual, iterate):
    block_rows = spikes.shape[0]
    neuron_cols = spikes.shape[1]
    basis_rows = basis_table(HISTORY, BASES)
    spike_low = spikes.astype(jnp.bfloat16)
    block_count = block_rows // HISTORY
    stacked = spike_low.reshape(block_count, HISTORY, neuron_cols)
    kernel_same = lag_kernel(basis_rows, HISTORY, 0)
    kernel_before = lag_kernel(basis_rows, HISTORY, HISTORY)
    current = jnp.einsum("bim,cmn->cinb", kernel_same, stacked, preferred_element_type=jnp.float32)
    tail_part = jnp.einsum(
        "bim,mn->inb", kernel_before, stacked[-1], preferred_element_type=jnp.float32
    )
    inner_part = jnp.einsum(
        "bim,cmn->cinb", kernel_before, stacked[:-1], preferred_element_type=jnp.float32
    )
    tail_terms = shifted(tail_part.astype(jnp.bfloat16), "tm", 1).astype(tail_part.dtype)
    own_terms = current + jnp.concatenate([tail_terms[None], inner_part], axis=0)
    features = own_terms.reshape(block_rows, neuron_cols * BASES).astype(jnp.bfloat16)
    direction_low = direction.astype(jnp.bfloat16)
    columns = features
    along_part = jnp.dot(
        columns,
        lax.all_gather(direction_low, "tm", axis=0, tiled=True),
        preferred_element_type=jnp.float32,
    )
    predictor_part = jnp.dot(features, weights, preferred_element_type=jnp.float32)
    tick_scale = exposure.astype(jnp.float32) / 8.0
    predictor_full, along_full = (
        lax.psum(predictor_part.astype(jnp.bfloat16), "nin").astype(jnp.float32),
        lax.psum(along_part.astype(jnp.bfloat16), "nin").astype(jnp.float32),
    )
    weighted = (tick_scale[:, None] * jnp.exp(predictor_full) * along_full).astype(jnp.bfloat16)
    columns = features
    gram = lax.psum_scatter(
        lax.dot_general(
            columns, weighted, (((0,), (0,)), ((), ())), preferred_element_type=jnp.float32
        ).astype(jnp.bfloat16),
        "tm",
        scatter_dimension=0,
        tiled=True,
    ).astype(jnp.float32)
    bin_total = block_rows * lax.axis_size("tm")
    curvature_prod = gram / bin_total + RIDGE_WEIGHT * direction
    old_norm, curvature = lax.psum(
        (jnp.sum(residual * residual, axis=0), jnp.sum(direction * curvature_prod, axis=0)),
        ("tm", "nin"),
    )
    step_size = old_norm / curvature
    new_iterate = iterate + step_size[None, :] * direction
    new_residual = residual - step_size[None, :] * curvature_prod
    new_norm = lax.psum(jnp.sum(new_residual * new_residual, axis=0), ("tm", "nin"))
    new_direction = new_residual + (new_norm / (old_norm + NORM_EPS))[None, :] * direction
    return (new_iterate, new_residual, new_direction)


def solution(mesh):
    in_specs = (
        P("tm", "nin"),
        P("tm"),
        P("nin", "nout"),
        P(("nin", "tm"), "nout"),
        P(("nin", "tm"), "nout"),
        P(("nin", "tm"), "nout"),
    )
    out_specs = (P(("nin", "tm"), "nout"), P(("nin", "tm"), "nout"), P(("nin", "tm"), "nout"))
    return jax.shard_map(
        per_device, mesh=mesh, in_specs=in_specs, out_specs=out_specs, check_vma=False
    )
```

profile of v0, /device:TPU:2, one launch (start us, length us, event | category | flops | bytes accessed | tf_op | source)
XLA Modules:
  0.0 800.1 jit_solution(18235166921538115580)
XLA Ops:
  7.2 0.0 all-gather.2.cloned.1.call-start
  7.2 1.8 convert_element_type.56
  9.0 0.0 all-gather.2.cloned.1.call-update
  9.0 0.0 all-reduce.4.cloned.1.call-start
  9.1 0.2 multiply_reduce_fusion.3
  9.3 0.1 divide_convert_fusion
  9.4 0.1 copy.17
  9.6 0.1 bitcast_clamp_fusion
  9.7 57.8 %gather_fusion.1 = bf16[16384,8]{1,0:T(8,128)(2,1)} fusion(bf16[8,128]{0,1:T(8,128)(2,1)S(1)} %copy.17, s32[16384]{0:T(1024)S(1)} %bitcast_clamp_fusion), kind=kCustom, calls=%fused_computation.1.clone | custom fusion | bytes 589824 | tf_op jit(solution)/shard_map/jit(_take)/gather | solution.py:40
  67.5 3.6 copy.20
  71.2 0.1 fusion.30
  71.3 1.1 fusion.1
  72.4 1.8 collective-permute-start
  74.2 57.8 %gather_fusion = bf16[16384,8]{1,0:T(8,128)(2,1)} fusion(bf16[8,128]{0,1:T(8,128)(2,1)S(1)} %copy.17, s32[16384]{0:T(1024)S(1)} %bitcast_clamp_fusion.1), kind=kCustom, calls=%fused_computation.clone | custom fusion | bytes 589824 | tf_op jit(solution)/shard_map/jit(_take)/gather | solution.py:40
  132.0 3.6 copy.18
  135.6 0.1 fusion.27
  135.7 0.3 convolution_bitcast_fusion
  136.0 0.1 bitcast_convert_fusion
  136.1 0.4 fusion
  136.5 2.1 copy.21
  138.6 2.8 convolution_convert_fusion.3
  141.4 3.0 convolution_convert_fusion.2
  144.4 0.0 all-reduce.4.cloned.1.call-update
  144.5 0.0 reduce-scatter.2.cloned.1.call-start
  144.5 85.0 %all-reduce.4.cloned.1.call-done = (bf16[256,512]{1,0:T(8,128)(2,1)}, bf16[256,512]{1,0:T(8,128)(2,1)}) async-done(((bf16[256,512]{1,0:T(8,128)(2,1)}, bf16[256,512]{1,0:T(8,128)(2,1)}), (bf16[256,512]{1,0:T(8,128)(2,1)}, bf16[256,512]{1,0:T(8,128)(2,1)})) %all-reduce.4.cloned.1.call-update) | async-done | bytes 524304 | tf_op jit(solution)/shard_map/psum | solution.py:74
  229.5 3.2 convolution_convert_fusion
  232.9 59.8 %reduce-scatter.2.cloned.1.call-done = bf16[128,512]{1,0:T(8,128)(2,1)} async-done(((bf16[2048,512]{1,0:T(8,128)(2,1)}), bf16[128,512]{1,0:T(8,128)(2,1)}) %reduce-scatter.2.cloned.1.call-update) | async-done | bytes 131088 | tf_op jit(solution)/shard_map/reduce_scatter | solution.py:78
  292.7 1.0 multiply_reduce_fusion.1
  293.6 250.6 %all-reduce = (f32[512]{0:T(512)S(1)}, f32[512]{0:T(512)S(1)}) all-reduce(f32[512]{0:T(512)S(1)} %multiply_reduce_fusion.2, f32[512]{0:T(512)S(1)} %multiply_reduce_fusion.1), channel_id=1, replica_groups=mesh['tm'=16,'nin'=8,'nout'=4] {'tm','nin'}, use_global_device_ids=true, to_apply=%region_1.2 | all-reduce | flops 1024 | bytes 8192 | tf_op jit(solution)/shard_map/psum | solution.py:88
  544.3 1.7 multiply_reduce_fusion
  546.0 246.8 %psum.39 = f32[512]{0:T(512)S(1)} all-reduce(f32[512]{0:T(512)S(1)} %get-tuple-element.8), channel_id=1, replica_groups=mesh['tm'=16,'nin'=8,'nout'=4] {'tm','nin'}, use_global_device_ids=true, to_apply=%region_9.11 | all-reduce | flops 512 | bytes 4096 | tf_op jit(solution)/shard_map/psum | solution.py:95
  792.8 0.8 multiply_add_fusion
  (28 shorter events, 0.2 us)
Async XLA Ops:
  7.2 131.5 %copy-start = (bf16[2048,512]{1,0:T(8,128)(2,1)S(1)}, bf16[2048,512]{1,0:T(8,128)(2,1)}, u32[]{:S(2)}) copy-start(bf16[2048,512]{1,0:T(8,128)(2,1)} %param.10) | copy-start | bytes 6291460
  7.2 134.2 %all-gather.2.cloned.1.call-start = ((), (), s32[]{:S(2)}) async-start(), calls=%async_computation.1 | async-start | bytes 2228224 | tf_op jit(solution)/shard_map/all_gather | solution.py:67
  9.0 220.5 %all-reduce.4.cloned.1.call-start = ((), (), s32[]{:S(2)}) async-start(), calls=%async_computation.3 | async-start | bytes 1048576 | tf_op jit(solution)/shard_map/psum | solution.py:74
  67.5 3.6 copy-start.5
  72.4 63.6 %collective-permute-start = (bf16[128,256,8]{1,0,2:T(8,128)(2,1)}, bf16[128,256,8]{1,0,2:T(8,128)(2,1)S(1)}, u32[]{:S(2)}, u32[]{:S(2)}) collective-permute-start(bf16[128,256,8]{1,0,2:T(8,128)(2,1)} %fusion.1), channel_id=1, source_target_pairs={{0,32},{32,64},{64,96},{96,128},{128,160},{160,192},{192,224},{224... | collective-permute-start | bytes 1572872 | tf_op jit(solution)/shard_map/ppermute | solution.py:16
  138.6 2.8 copy-start.2
  141.4 3.1 copy-start.7
  144.5 148.2 %reduce-scatter.2.cloned.1.call-start = ((), (), s32[]{:S(2)}) async-start(), calls=%async_computation.2 | async-start | bytes 2228224 | tf_op jit(solution)/shard_map/reduce_scatter | solution.py:78
  229.5 3.3 copy-start.4
  232.8 59.9 %copy-start.1 = (f32[128,512]{1,0:T(8,128)S(1)}, f32[128,512]{1,0:T(8,128)}, u32[]{:S(2)}) copy-start(f32[128,512]{1,0:T(8,128)} %param.11) | copy-start | bytes 786436
  232.8 311.5 %copy-start.6 = (f32[128,512]{1,0:T(8,128)S(1)}, f32[128,512]{1,0:T(8,128)}, u32[]{:S(2)}) copy-start(f32[128,512]{1,0:T(8,128)} %param.13) | copy-start | bytes 786436
  546.0 247.6 %copy-start.3 = (f32[128,512]{1,0:T(8,128)}, f32[128,512]{1,0:T(8,128)S(1)}, u32[]{:S(2)}) copy-start(f32[128,512]{1,0:T(8,128)S(1)} %get-tuple-element.9) | copy-start | bytes 786436
Sparse Core Ops, SparseCore 0:
  10.7 46.5 all-gather.1
  144.6 84.9 all-reduce.3
  232.9 59.6 reduce-scatter.1
where the time goes:
time: 800 us
  blocking collectives  497 us (62%)
  waiting for transfers between devices  145 us (18%)
  local copies, waits for them, and re-layouts  125 us (16%)
  between operations  13.9 us (2%)
  matrix products  10.8 us (1%)
    psum x1, blocking collectives, per_device(): lax.psum((jnp.sum(residual * residual, axis=0), jnp.sum(direction * curva...  251 us
    psum x1, blocking collectives, per_device(): lax.psum(jnp.sum(new_residual * new_residual, axis=0), ('tm', 'nin'))  247 us
    gather x4, local copies, waits for them, and re-layouts, lag_kernel(): jnp.take(basis_rows.T, take_index, axis=1)  123 us
    psum x1, waiting for transfers between devices, per_device(): lax.psum(along_part.astype(jnp.bfloat16), 'nin').astype(jnp.float32)  85 us
    reduce_scatter x1, waiting for transfers between devices, per_device(): lax.psum_scatter(lax.dot_general(columns, weighted, (((0,), (0,)), ((), (...  59.8 us
  transfers between devices with their start and end apart: 4, of which 2 were waited for; matrix products, arithmetic and copies ran while one was open for 16% of the time, Pallas kernels for 0%

commit v1 on v0

--- a/solution.py
+++ b/solution.py
@@ -92,7 +92,9 @@
     step_size = old_norm / curvature
     new_iterate = iterate + step_size[None, :] * direction
     new_residual = residual - step_size[None, :] * curvature_prod
-    new_norm = lax.psum(jnp.sum(new_residual * new_residual, axis=0), ("tm", "nin"))
+    new_norm = jnp.sum(new_residual * new_residual, axis=0)
+    for mesh_axis in ("tm", "nin"):
+        new_norm = lax.psum(new_norm, mesh_axis)
     new_direction = new_residual + (new_norm / (old_norm + NORM_EPS))[None, :] * direction
     return (new_iterate, new_residual, new_direction)
 

time: 800 us -> 591 us (0.74)
  the two profiles are of different devices: /device:TPU:2 before, /device:TPU:6 now
where the time goes in v1:
time: 591 us; the launch traced here: 590 us
  blocking collectives  288 us (49%)
  waiting for transfers between devices  145 us (25%)
  local copies, waits for them, and re-layouts  124 us (21%)
  between operations  13.9 us (2%)
  matrix products  10.8 us (2%)
  other arithmetic  6.02 us (1%)
    psum x1, blocking collectives, per_device(): lax.psum((jnp.sum(residual * residual, axis=0), jnp.sum(direction * curva...  251 us
    gather x4, local copies, waits for them, and re-layouts, lag_kernel(): jnp.take(basis_rows.T, take_index, axis=1)  122 us
    psum x1, waiting for transfers between devices, per_device(): lax.psum(along_part.astype(jnp.bfloat16), 'nin').astype(jnp.float32)  85 us
    reduce_scatter x1, waiting for transfers between devices, per_device(): lax.psum_scatter(lax.dot_general(columns, weighted, (((0,), (0,)), ((), (...  59.8 us
    psum x2, blocking collectives, per_device(): new_norm = lax.psum(new_norm, mesh_axis)  37.7 us
  transfers between devices with their start and end apart: 4, of which 2 were waited for; matrix products, arithmetic and copies ran while one was open for 22% of the time, Pallas kernels for 0%

profile of v1, /device:TPU:6, one launch (start us, length us, event | category | flops | bytes accessed | tf_op | source)
XLA Modules:
  0.0 590.1 jit_solution(488128586828846715)
XLA Ops:
  7.2 0.0 all-gather.2.cloned.1.call-start
  7.2 1.8 convert_element_type.56
  9.0 0.0 all-gather.2.cloned.1.call-update
  9.0 0.0 all-reduce.4.cloned.1.call-start
  9.1 0.2 multiply_reduce_fusion.3
  9.3 0.1 divide_convert_fusion
  9.4 0.1 copy.17
  9.6 0.1 bitcast_clamp_fusion
  9.7 57.4 %gather_fusion.1 = bf16[16384,8]{1,0:T(8,128)(2,1)} fusion(bf16[8,128]{0,1:T(8,128)(2,1)S(1)} %copy.17, s32[16384]{0:T(1024)S(1)} %bitcast_clamp_fusion), kind=kCustom, calls=%fused_computation.1.clone | custom fusion | bytes 589824 | tf_op jit(solution)/shard_map/jit(_take)/gather | solution.py:40
  67.1 3.6 copy.20
  70.8 0.1 fusion.30
  70.9 1.1 fusion.1
  72.0 1.8 collective-permute-start
  73.8 57.4 %gather_fusion = bf16[16384,8]{1,0:T(8,128)(2,1)} fusion(bf16[8,128]{0,1:T(8,128)(2,1)S(1)} %copy.17, s32[16384]{0:T(1024)S(1)} %bitcast_clamp_fusion.1), kind=kCustom, calls=%fused_computation.clone | custom fusion | bytes 589824 | tf_op jit(solution)/shard_map/jit(_take)/gather | solution.py:40
  131.2 3.6 copy.18
  134.7 0.1 fusion.27
  134.8 0.3 convolution_bitcast_fusion
  135.1 0.1 bitcast_convert_fusion
  135.2 0.4 fusion
  135.6 2.1 copy.21
  137.7 2.8 convolution_convert_fusion.3
  140.5 3.1 convolution_convert_fusion.2
  143.6 0.0 reduce-scatter.2.cloned.1.call-start
  143.7 85.0 %all-reduce.4.cloned.1.call-done = (bf16[256,512]{1,0:T(8,128)(2,1)}, bf16[256,512]{1,0:T(8,128)(2,1)}) async-done(((bf16[256,512]{1,0:T(8,128)(2,1)}, bf16[256,512]{1,0:T(8,128)(2,1)}), (bf16[256,512]{1,0:T(8,128)(2,1)}, bf16[256,512]{1,0:T(8,128)(2,1)})) %all-reduce.4.cloned.1.call-update) | async-done | bytes 524304 | tf_op jit(solution)/shard_map/psum | solution.py:74
  228.6 3.2 convolution_convert_fusion
  231.9 59.8 %reduce-scatter.2.cloned.1.call-done = bf16[128,512]{1,0:T(8,128)(2,1)} async-done(((bf16[2048,512]{1,0:T(8,128)(2,1)}), bf16[128,512]{1,0:T(8,128)(2,1)}) %reduce-scatter.2.cloned.1.call-update) | async-done | bytes 131088 | tf_op jit(solution)/shard_map/reduce_scatter | solution.py:78
  291.7 1.0 multiply_reduce_fusion.1
  292.7 250.7 %all-reduce = (f32[512]{0:T(512)S(1)}, f32[512]{0:T(512)S(1)}) all-reduce(f32[512]{0:T(512)S(1)} %multiply_reduce_fusion.2, f32[512]{0:T(512)S(1)} %multiply_reduce_fusion.1), channel_id=1, replica_groups=mesh['tm'=16,'nin'=8,'nout'=4] {'tm','nin'}, use_global_device_ids=true, to_apply=%region_1.2 | all-reduce | flops 1024 | bytes 8192 | tf_op jit(solution)/shard_map/psum | solution.py:88
  543.4 1.7 multiply_reduce_fusion
  545.1 23.5 %psum.46 = f32[512]{0:T(512)S(1)} all-reduce(f32[512]{0:T(512)S(1)} %get-tuple-element.8), channel_id=1, replica_groups=mesh['tm'=16,'nin'=8,'nout'=4] {'tm'}, use_global_device_ids=true, to_apply=%region_9.11 | all-reduce | flops 512 | bytes 4096 | tf_op jit(solution)/shard_map/psum | solution.py:97
  568.6 14.2 %psum.47 = f32[512]{0:T(512)S(1)} all-reduce(f32[512]{0:T(512)S(1)} %psum.46), channel_id=1, replica_groups=mesh['tm'=16,'nin'=8,'nout'=4] {'nin'}, use_global_device_ids=true, to_apply=%region_10.12 | all-reduce | flops 512 | bytes 4096 | tf_op jit(solution)/shard_map/psum | solution.py:97
  582.8 0.8 multiply_add_fusion
  (29 shorter events, 0.2 us)
Async XLA Ops:
  7.2 130.6 %copy-start = (bf16[2048,512]{1,0:T(8,128)(2,1)S(1)}, bf16[2048,512]{1,0:T(8,128)(2,1)}, u32[]{:S(2)}) copy-start(bf16[2048,512]{1,0:T(8,128)(2,1)} %param.10) | copy-start | bytes 6291460
  7.2 133.3 %all-gather.2.cloned.1.call-start = ((), (), s32[]{:S(2)}) async-start(), calls=%async_computation.1 | async-start | bytes 2228224 | tf_op jit(solution)/shard_map/all_gather | solution.py:67
  9.0 219.6 %all-reduce.4.cloned.1.call-start = ((), (), s32[]{:S(2)}) async-start(), calls=%async_computation.3 | async-start | bytes 1048576 | tf_op jit(solution)/shard_map/psum | solution.py:74
  67.1 3.6 copy-start.5
  72.0 63.1 %collective-permute-start = (bf16[128,256,8]{1,0,2:T(8,128)(2,1)}, bf16[128,256,8]{1,0,2:T(8,128)(2,1)S(1)}, u32[]{:S(2)}, u32[]{:S(2)}) collective-permute-start(bf16[128,256,8]{1,0,2:T(8,128)(2,1)} %fusion.1), channel_id=1, source_target_pairs={{0,32},{32,64},{64,96},{96,128},{128,160},{160,192},{192,224},{224... | collective-permute-start | bytes 1572872 | tf_op jit(solution)/shard_map/ppermute | solution.py:16
  137.7 2.8 copy-start.2
  140.5 3.1 copy-start.7
  143.6 148.1 %reduce-scatter.2.cloned.1.call-start = ((), (), s32[]{:S(2)}) async-start(), calls=%async_computation.2 | async-start | bytes 2228224 | tf_op jit(solution)/shard_map/reduce_scatter | solution.py:78
  228.6 3.3 copy-start.4
  231.8 59.9 %copy-start.1 = (f32[128,512]{1,0:T(8,128)S(1)}, f32[128,512]{1,0:T(8,128)}, u32[]{:S(2)}) copy-start(f32[128,512]{1,0:T(8,128)} %param.11) | copy-start | bytes 786436
  231.8 311.5 %copy-start.6 = (f32[128,512]{1,0:T(8,128)S(1)}, f32[128,512]{1,0:T(8,128)}, u32[]{:S(2)}) copy-start(f32[128,512]{1,0:T(8,128)} %param.13) | copy-start | bytes 786436
  545.1 38.4 %copy-start.3 = (f32[128,512]{1,0:T(8,128)}, f32[128,512]{1,0:T(8,128)S(1)}, u32[]{:S(2)}) copy-start(f32[128,512]{1,0:T(8,128)S(1)} %get-tuple-element.9) | copy-start | bytes 786436
Sparse Core Ops, SparseCore 0:
  10.7 46.4 all-gather.1
  143.7 84.8 all-reduce.3
  232.0 59.6 reduce-scatter.1
